TPU v7x, 256 devices: a whole 4x4x8 slice. The times are simulated.
256 devices in a mesh: context: 32 (over z, y_lo, core), tensor: 8 (over y_hi, x).
Axes of the slice: x: 4, y: 4 (y_hi: 2, y_lo: 2; y = y_hi * 2 + y_lo), z: 8, core: 2. Of those that a mesh axis runs over, the one named last changes fastest.
Arguments:
- layer_input: bfloat16 [4096, 8192], P(('context', 'tensor')), may hold values from -24 to 24
- query_stream: bfloat16 [4096, 4096], P('context', 'tensor'), may hold values from -6 to 6
- key_stream: bfloat16 [4096, 4096], P('context', 'tensor'), may hold values from -6 to 6
- value_stream: bfloat16 [4096, 4096], P('context', 'tensor'), may hold values from -6 to 6
- output_grad: bfloat16 [4096, 4096], P('context', 'tensor'), may hold values from -6 to 6
- filter_taps: bfloat16 [4096, 128], P('tensor'), may hold values from -0.5 to 0.5
- skip_gain: float32 [4096], P('tensor'), may hold values from 0.5 to 1.5
- value_weight: bfloat16 [8192, 4096], P(None, 'tensor'), may hold values from -0.0625 to 0.0625
Outputs:
- query_grad: bfloat16 [4096, 4096], P('context', 'tensor')
- key_grad: bfloat16 [4096, 4096], P('context', 'tensor')
- value_grad: bfloat16 [4096, 4096], P('context', 'tensor')
- filter_grad: float32 [4096, 128], P('tensor')
- skip_grad: float32 [4096], P('tensor')
- input_grad: bfloat16 [4096, 8192], P(('context', 'tensor'))
- weight_grad: float32 [8192, 4096], P('context', 'tensor')
All inputs are finite; a program needn't handle non-finite values.
Results may differ from a plain program's by a relative error of at most 0.015.
Values may be sent and summed in bfloat16 or wider, within the bound.
A program may use at most 128 MiB of HBM per device.

v0:
```python
import jax
import jax.numpy as jnp
from jax import lax
from jax.sharding import PartitionSpec as P


def passed_along(value, axis, steps):
    count = lax.axis_size(axis)
    first, last = (max(0, -steps), min(count, count - steps))
    return lax.ppermute(value, axis, [(source, source + steps) for source in range(first, last)])


def lag_table(taps_count, block_rows, span):
    lag_index = jnp.arange(taps_count, dtype=jnp.int32)[:, None, None]
    row_index = jnp.arange(block_rows, dtype=jnp.int32)[None, :, None]
    col_index = jnp.arange(span, dtype=jnp.int32)[None, None, :]
    return (row_index + taps_count - col_index == lag_index).astype(jnp.bfloat16)


def local(
    layer_input,
    query_stream,
    key_stream,
    value_stream,
    output_grad,
    filter_taps,
    skip_gain,
    value_weight,
):
    length, chans = query_stream.shape
    taps_count = filter_taps.shape[1]
    rim = taps_count - 1
    block_rows = 64
    blocks = length // block_rows
    inner = (key_stream.astype(jnp.float32) * value_stream.astype(jnp.float32)).astype(jnp.bfloat16)
    delta = (output_grad.astype(jnp.float32) * query_stream.astype(jnp.float32)).astype(
        jnp.bfloat16
    )
    before = passed_along(inner[length - rim :], "context", 1)
    after = passed_along(delta[:rim], "context", -1)
    zero_row = jnp.zeros((1, chans), jnp.bfloat16)
    inner_ext = jnp.concatenate([zero_row, before, inner], axis=0).T
    delta_ext = jnp.concatenate([delta, after, zero_row], axis=0).T
    selector = lag_table(taps_count, block_rows, 3 * block_rows)
    banded = jnp.einsum(
        "cj,jts->cts", filter_taps, selector, preferred_element_type=jnp.float32
    ).astype(jnp.bfloat16)
    inner_blocks = inner_ext.reshape(chans, blocks + 2, block_rows)
    window = jnp.concatenate(
        [inner_blocks[:, :blocks], inner_blocks[:, 1 : blocks + 1], inner_blocks[:, 2:]], axis=2
    )
    filtered = jnp.einsum(
        "cts,cbs->cbt", banded, window, preferred_element_type=jnp.float32
    ).reshape(chans, length)
    gain_column = skip_gain[:, None]
    mixed = filtered + gain_column * inner.T.astype(jnp.float32)
    query_grad = (output_grad.astype(jnp.float32) * mixed.T).astype(jnp.bfloat16)
    delta_blocks = delta_ext.reshape(chans, blocks + 2, block_rows)
    spread = jnp.einsum("cts,cbt->cbs", banded, delta_blocks, preferred_element_type=jnp.float32)
    backward = (
        spread[:, :blocks, 2 * block_rows :]
        + spread[:, 1 : blocks + 1, block_rows : 2 * block_rows]
        + spread[:, 2:, :block_rows]
    )
    backward = backward.reshape(chans, length) + gain_column * delta.T.astype(jnp.float32)
    back_rows = backward.T
    key_grad = (back_rows * value_stream.astype(jnp.float32)).astype(jnp.bfloat16)
    value_grad = (back_rows * key_stream.astype(jnp.float32)).astype(jnp.bfloat16)
    outer_sums = jnp.einsum(
        "cbt,cbs->cts", delta_blocks[:, :blocks], window, preferred_element_type=jnp.float32
    )
    taps_local = jnp.einsum(
        "cts,jts->cj",
        outer_sums,
        selector.astype(jnp.float32),
        precision=lax.Precision.HIGHEST,
        preferred_element_type=jnp.float32,
    )
    skip_local = jnp.sum(delta.astype(jnp.float32) * inner.astype(jnp.float32), axis=0)
    filter_grad, skip_grad = lax.psum((taps_local, skip_local), "context")
    input_grad = lax.psum_scatter(
        lax.dot_general(
            value_grad, value_weight, (((1,), (1,)), ((), ())), preferred_element_type=jnp.float32
        ).astype(jnp.bfloat16),
        "tensor",
        scatter_dimension=0,
        tiled=True,
    )
    gathered = lax.all_gather(layer_input, "tensor", axis=0, tiled=True)
    weight_grad = lax.psum_scatter(
        lax.dot_general(
            gathered, value_grad, (((0,), (0,)), ((), ())), preferred_element_type=jnp.float32
        ),
        "context",
        scatter_dimension=0,
        tiled=True,
    )
    return (query_grad, key_grad, value_grad, filter_grad, skip_grad, input_grad, weight_grad)


def solution(mesh):
    placed = (
        P(("context", "tensor"), None),
        P("context", "tensor"),
        P("context", "tensor"),
        P("context", "tensor"),
        P("context", "tensor"),
        P("tensor", None),
        P("tensor"),
        P(None, "tensor"),
    )
    return jax.shard_map(
        local,
        mesh=mesh,
        in_specs=placed,
        out_specs=(
            P("context", "tensor"),
            P("context", "tensor"),
            P("context", "tensor"),
            P("tensor", None),
            P("tensor"),
            P(("context", "tensor"), None),
            P("context", "tensor"),
        ),
        check_vma=False,
    )
```

profile of v0, /device:TPU:1, one launch (start us, length us, event | category | flops | bytes accessed | tf_op | source)
XLA Modules:
  0.0 596.1 jit_solution(2453043291420033951)
XLA Ops:
  7.2 1.2 fusion.18
  8.4 5.1 collective-permute-start.1
  13.6 1.9 collective-permute-start
  15.6 0.0 reduce-scatter.5.cloned.1.call-start
  15.7 0.1 iota_subtract_fusion
  15.7 6.6 %convert_bitcast_fusion = bf16[512,64,192]{0,2,1:T(8,128)(2,1)} fusion(s32[64,192]{1,0:T(8,128)S(1)} %iota_subtract_fusion, bf16[512,128]{1,0:T(8,128)(2,1)S(1)} %copy-done), kind=kOutput, calls=%fused_computation.3 | convolution fusion | flops 1618477056 | bytes 12763136 | tf_op jit(solution)/shard_map/cj,jts->cts/dot_general | solution.py:45
  22.3 24.2 %copy.25 = bf16[512,64,192]{2,1,0:T(8,128)(2,1)} copy(bf16[512,64,192]{0,2,1:T(8,128)(2,1)} %convert_bitcast_fusion) | data formatting | bytes 25165824 | tf_op jit(solution)/shard_map/convert_element_type | solution.py:47
  46.5 0.1 pad_maximum_fusion.2
  46.6 0.3 copy.27
  46.9 8.0 %fusion.25 = f32[512,4,192]{2,1,0:T(4,128)S(1)} fusion(bf16[512,4,64]{2,1,0:T(4,128)(2,1)S(1)} %copy.27, bf16[512,64,192]{2,1,0:T(8,128)(2,1)} %copy.25), kind=kOutput, calls=%fused_computation.40 | convolution fusion | flops 50331648 | bytes 14417920 | tf_op jit(solution)/shard_map/cts,cbt->cbs/dot_general | solution.py:59
  55.0 0.7 slice_add_fusion
  55.6 0.2 copy.29
  55.9 0.2 copy.35
  56.0 0.2 copy.34
  56.2 0.2 copy.33
  56.4 10.3 %fusion.21 = f32[512,2,64]{2,1,0:T(2,128)S(1)} fusion(bf16[512,64,192]{2,1,0:T(8,128)(2,1)} %copy.25, bf16[512,2,64]{2,1,0:T(2,128)(2,1)S(1)} %copy.35, bf16[512,2,64]{2,1,0:T(2,128)(2,1)S(1)} %copy.34, bf16[512,2,64]{2,1,0:T(2,128)(2,1)S(1)} %copy.33), kind=kOutput, calls=%fused_computation.38 | convolution fusion | flops 26345472 | bytes 13238272 | tf_op jit(solution)/shard_map/cts,cbs->cbt/dot_general | solution.py:52
  66.7 0.2 copy.26
  67.0 0.8 fusion.9
  67.8 9.1 %all-gather.2.cloned.1.call-done = bf16[128,8192]{1,0:T(8,128)(2,1)} async-done(((bf16[16,8192]{1,0:T(8,128)(2,1)}), bf16[128,8192]{1,0:T(8,128)(2,1)}) %all-gather.2.cloned.1.call-update) | async-done | bytes 2097168 | tf_op jit(solution)/shard_map/all_gather | solution.py:89
  77.0 9.7 %convolution_bitcast_fusion = f32[8192,512]{0,1:T(8,128)} fusion(bf16[128,512]{1,0:T(8,128)(2,1)S(1)} %get-tuple-element.34, bf16[128,8192]{1,0:T(8,128)(2,1)} %all-gather.2.cloned.1.call-done), kind=kOutput, calls=%fused_computation.2 | convolution fusion | flops 1073741824 | bytes 19005440 | tf_op jit(solution)/shard_map/dot_general | solution.py:91
  86.7 0.2 all-reduce.2.cloned.1.call-start
  86.9 0.2 copy.31
  87.1 13.7 %fusion.20 = f32[512,64,192]{2,1,0:T(8,128)} fusion(bf16[512,2,64]{2,1,0:T(2,128)(2,1)S(1)} %copy.31, bf16[512,2,64]{2,1,0:T(2,128)(2,1)S(1)} %copy.35, bf16[512,2,64]{2,1,0:T(2,128)(2,1)S(1)} %copy.34, bf16[512,2,64]{2,1,0:T(2,128)(2,1)S(1)} %copy.33), kind=kOutput, calls=%fused_computation.37 | convolution fusion | flops 26345472 | bytes 25690112 | tf_op jit(solution)/shard_map/cbt,cbs->cts/dot_general | solution.py:69
  100.8 31.2 %fusion.4 = f32[512,128]{1,0:T(8,128)} fusion(s32[64,192]{1,0:T(8,128)S(1)} %iota_subtract_fusion, f32[512,64,192]{2,1,0:T(8,128)} %fusion.20), kind=kOutput, calls=%fused_computation.8 | convolution fusion | flops 9665249280 | bytes 25477120 | tf_op jit(solution)/shard_map/cts,jts->cj/dot_general | solution.py:72
  132.0 0.0 reduce-scatter.3.cloned.1.call-start
  132.0 7.6 %convolution_convert_fusion = bf16[128,8192]{1,0:T(8,128)(2,1)} fusion(bf16[128,512]{1,0:T(8,128)(2,1)S(1)} %get-tuple-element.34, bf16[8192,512]{1,0:T(8,128)(2,1)} %param.15), kind=kOutput, calls=%fused_computation.4 | convolution fusion | flops 1074790400 | bytes 10616832 | tf_op jit(solution)/shard_map/dot_general | solution.py:82
  139.6 55.9 %psum.15 = f32[512]{0:T(512)} all-reduce(f32[512]{0:T(512)S(1)} %get-tuple-element.21), channel_id=1, replica_groups=mesh['context'=32,'tensor'=8] {'context'}, use_global_device_ids=true, to_apply=%region_2.0 | all-reduce | flops 512 | bytes 4096 | tf_op jit(solution)/shard_map/psum | solution.py:80
  195.5 81.9 %reduce-scatter.5.cloned.1.call-done = f32[256,512]{0,1:T(8,128)} async-done(((f32[8192,512]{0,1:T(8,128)}), f32[256,512]{0,1:T(8,128)}) %reduce-scatter.5.cloned.1.call-update) | async-done | bytes 524304 | tf_op jit(solution)/shard_map/reduce_scatter | solution.py:90
  277.4 2.0 copy.30
  279.5 224.1 %all-reduce.2.cloned.1.call-done = f32[512,128]{1,0:T(8,128)} async-done(((f32[512,128]{1,0:T(8,128)}), f32[512,128]{1,0:T(8,128)}) %all-reduce.2.cloned.1.call-update) | async-done | bytes 262160 | tf_op jit(solution)/shard_map/psum | solution.py:80
  503.6 84.3 %reduce-scatter.3.cloned.1.call-done = bf16[16,8192]{1,0:T(8,128)(2,1)} async-done(((bf16[128,8192]{1,0:T(8,128)(2,1)}), bf16[16,8192]{1,0:T(8,128)(2,1)}) %reduce-scatter.3.cloned.1.call-update) | async-done | bytes 262160 | tf_op jit(solution)/shard_map/reduce_scatter | solution.py:81
  587.9 1.7 copy.41
  (26 shorter events, 0.2 us)
Async XLA Ops:
  7.2 8.6 %copy-start = (bf16[512,128]{1,0:T(8,128)(2,1)S(1)}, bf16[512,128]{1,0:T(8,128)(2,1)}, u32[]{:S(2)}) copy-start(bf16[512,128]{1,0:T(8,128)(2,1)} %param.13) | copy-start | bytes 393220
  7.2 69.8 %all-gather.2.cloned.1.call-start = ((), (), s32[]{:S(2)}) async-start(), calls=%async_computation.4 | async-start | bytes 2359296 | tf_op jit(solution)/shard_map/all_gather | solution.py:89
  8.4 38.1 %collective-permute-start.1 = (bf16[127,512]{1,0:T(8,128)(2,1)S(1)}, bf16[127,512]{1,0:T(8,128)(2,1)S(1)}, u32[]{:S(2)}, u32[]{:S(2)}) collective-permute-start(bf16[127,512]{1,0:T(8,128)(2,1)S(1)} %bitcast.63), channel_id=1, source_target_pairs={{8,0},{16,8},{24,16},{32,24},{40,32},{48,40},{56,48},{64,56},{72,6... | collective-permute-start | bytes 390152 | tf_op jit(solution)/shard_map/ppermute | solution.py:10
  13.6 32.9 %collective-permute-start = (bf16[127,512]{1,0:T(8,128)(2,1)S(1)}, bf16[127,512]{1,0:T(8,128)(2,1)S(1)}, u32[]{:S(2)}, u32[]{:S(2)}) collective-permute-start(bf16[127,512]{1,0:T(8,128)(2,1)S(1)} %slice.36), channel_id=1, source_target_pairs={{0,8},{8,16},{16,24},{24,32},{32,40},{40,48},{48,56},{56,64},{64,7... | collective-permute-start | bytes 390152 | tf_op jit(solution)/shard_map/ppermute | solution.py:10
  15.6 261.9 %reduce-scatter.5.cloned.1.call-start = ((), (), s32[]{:S(2)}) async-start(), calls=%async_computation.5 | async-start | bytes 17301504 | tf_op jit(solution)/shard_map/reduce_scatter | solution.py:90
  56.4 10.6 %copy-start.3 = (bf16[128,512]{1,0:T(8,128)(2,1)S(1)}, bf16[128,512]{1,0:T(8,128)(2,1)}, u32[]{:S(2)}) copy-start(bf16[128,512]{1,0:T(8,128)(2,1)} %param.10) | copy-start | bytes 393220
  56.4 10.6 %copy-start.4 = (bf16[128,512]{1,0:T(8,128)(2,1)S(1)}, bf16[128,512]{1,0:T(8,128)(2,1)}, u32[]{:S(2)}) copy-start(bf16[128,512]{1,0:T(8,128)(2,1)} %param.12) | copy-start | bytes 393220
  56.4 10.6 %copy-start.5 = (bf16[128,512]{1,0:T(8,128)(2,1)S(1)}, bf16[128,512]{1,0:T(8,128)(2,1)}, u32[]{:S(2)}) copy-start(bf16[128,512]{1,0:T(8,128)(2,1)} %param.11) | copy-start | bytes 393220
  56.4 10.6 %copy-start.6 = (f32[512]{0:T(512)S(1)}, f32[512]{0:T(512)}, u32[]{:S(2)}) copy-start(f32[512]{0:T(512)} %param.14) | copy-start | bytes 6148
  67.8 64.2 %copy-start.2 = (bf16[128,512]{1,0:T(8,128)(2,1)}, bf16[128,512]{1,0:T(8,128)(2,1)S(1)}, u32[]{:S(2)}) copy-start(bf16[128,512]{1,0:T(8,128)(2,1)S(1)} %get-tuple-element.34) | copy-start | bytes 393220
  86.7 416.9 %all-reduce.2.cloned.1.call-start = ((), (), s32[]{:S(2)}) async-start(), calls=%async_computation.2 | async-start | bytes 524288 | tf_op jit(solution)/shard_map/psum | solution.py:80
  100.8 488.8 %copy-start.1 = (bf16[512,128]{1,0:T(8,128)(2,1)S(1)}, bf16[512,128]{1,0:T(8,128)(2,1)}, u32[]{:S(2)}) copy-start(bf16[512,128]{1,0:T(8,128)(2,1)} %param.13) | copy-start | bytes 393220
  132.0 456.0 %reduce-scatter.3.cloned.1.call-start = ((), (), s32[]{:S(2)}) async-start(), calls=%async_computation.3 | async-start | bytes 2359296 | tf_op jit(solution)/shard_map/reduce_scatter | solution.py:81
Sparse Core Ops, SparseCore 0:
  15.7 61.2 all-gather.1
  86.8 190.6 reduce-scatter.4
  280.6 222.9 all-reduce.1
  508.6 79.2 reduce-scatter.2
where the time goes:
time: 597 us; the launch traced here: 596 us
  waiting for transfers between devices  400 us (67%)
  matrix products  87 us (15%)
  blocking collectives  55.9 us (9%)
  local copies, waits for them, and re-layouts  29.4 us (5%)
  between operations  14 us (2%)
  starting transfers between devices  7.41 us (1%)
    psum x1, waiting for transfers between devices, local(): filter_grad, skip_grad = lax.psum((taps_local, skip_local), 'context')  224 us
    reduce_scatter x1, waiting for transfers between devices, local(): lax.psum_scatter(lax.dot_general(value_grad, value_weight, (((1,), (1,)),...  84.3 us
    reduce_scatter x1, waiting for transfers between devices, local(): lax.psum_scatter(lax.dot_general(gathered, value_grad, (((0,), (0,)), (()...  81.9 us
    psum x1, blocking collectives, local(): filter_grad, skip_grad = lax.psum((taps_local, skip_local), 'context')  55.9 us
    dot_general x1, matrix products, local(): jnp.einsum('cts,jts->cj', outer_sums, selector.astype(jnp.float32), preci...  31.2 us
    convert_element_type x1, local copies, waits for them, and re-layouts, local(): banded = jnp.einsum('cj,jts->cts', filter_taps, selector, preferred_eleme...  24.2 us
    dot_general x1, matrix products, local(): jnp.einsum('cbt,cbs->cts', delta_blocks[:, :blocks], window, preferred_el...  13.7 us
  transfers between devices with their start and end apart: 6, of which 4 were waited for; matrix products, arithmetic and copies ran while one was open for 18% of the time, Pallas kernels for 0%

commit v1 on v0

v1 whole, which is shorter than its diff:
```python
import functools

import jax
import jax.numpy as jnp
from jax import lax
from jax.experimental import pallas as pl
from jax.experimental.pallas import tpu as pltpu
from jax.sharding import PartitionSpec as P

MESH = pl.DeviceIdType.MESH
BF16 = jnp.bfloat16
F32 = jnp.float32

NZ, NYL, NCORE, NYH, NX = 8, 2, 2, 2, 4
NQ = NZ * NYL
NT = NYH * NX
TAPS = 128
ROWS = 128
CH = 512
SUB = 16
D = 8192
WIDE = D // NQ
CHUNKS = 4
CCOLS = D // CHUNKS


def kernel(
    x_hbm, q_hbm, k_hbm, v_hbm, g_hbm, taps_hbm, gain_hbm, w_hbm,
    qg_hbm, kg_hbm, vg_hbm, fg_hbm, sg_hbm, ig_hbm, wg_hbm,
    qv, kv, vv, gv, taps_v, gain_v, w_v,
    inner, delta, halo_d, halo_i, tapst, dext, iext, d8, e8, back,
    qgv, kgv, xa, ga, tpart, trecv, ig, wacc, wrecv, wout,
    fpart, fcore, fsum, frs, ffull, fgt, sgv,
    in_sems, out_sems, halo_s, halo_r, a2a_s, a2a_r, ag_s, ag_r, b_s, b_r, c_s, c_r,
    core_s, core_r, rs_s, rs_r, fa_s, fa_r,
):
    con = lax.axis_index("context")
    ten = lax.axis_index("tensor")
    z, yl, core = con // 4, (con // 2) % 2, con % 2
    yh, x = ten // 4, ten % 4
    q = con // 2

    def at(zz, yy, cc):
        return (zz % NZ) * 4 + (yy % 2) * 2 + cc % 2

    def ten_at(hh, xx):
        return (hh % 2) * 4 + xx % 4

    def remote(src, dst, ss, rs, device):
        return pltpu.make_async_remote_copy(
            src_ref=src, dst_ref=dst, send_sem=ss, recv_sem=rs, device_id=device, device_id_type=MESH
        )

    loads = [
        pltpu.make_async_copy(src, dst, in_sems.at[i])
        for i, (src, dst) in enumerate(
            [(k_hbm, kv), (v_hbm, vv), (g_hbm, gv), (q_hbm, qv), (taps_hbm, taps_v), (gain_hbm, gain_v), (w_hbm, w_v)]
        )
    ]
    for copy in loads:
        copy.start()

    barrier = pltpu.get_barrier_semaphore()
    above = (con + 1) % 32
    below = (con + 31) % 32

    def greet(device):
        pl.semaphore_signal(barrier, inc=1, device_id=device, device_id_type=MESH)

    greet((above, ten))
    greet((below, ten))
    greet((at(z, yl, core + 1), ten))

    def greet_q(i, carry):
        greet((at(z + i // 2, yl + i % 2, core), ten))
        return carry

    lax.fori_loop(1, NQ, greet_q, 0)

    def greet_t(i, carry):
        greet((con, (ten + i) % NT))
        return carry

    lax.fori_loop(1, NT, greet_t, 0)

    loads[0].wait()
    loads[1].wait()
    loads[2].wait()
    loads[3].wait()
    inner[...] = (kv[...].astype(F32) * vv[...].astype(F32)).astype(BF16)
    delta[...] = (gv[...].astype(F32) * qv[...].astype(F32)).astype(BF16)
    dext[pl.ds(0, ROWS), :] = delta[...].astype(F32)
    iext[pl.ds(ROWS, ROWS), :] = inner[...].astype(F32)

    pl.semaphore_wait(barrier, 3 + (NQ - 1) + (NT - 1))

    halo_delta = remote(delta, halo_d, halo_s.at[0], halo_r.at[0], (below, ten))
    halo_inner = remote(inner, halo_i, halo_s.at[1], halo_r.at[1], (above, ten))
    halo_delta.start()
    halo_inner.start()

    own_x = pltpu.make_async_copy(
        x_hbm.at[:, pl.ds(pl.multiple_of(q * WIDE, WIDE), WIDE)], xa.at[q, ten], in_sems.at[7]
    )
    own_x.start()

    def a2a_copy(i):
        dest = ((z + i // 2) % NZ) * 2 + (yl + i % 2) % 2
        return remote(
            x_hbm.at[:, pl.ds(pl.multiple_of(dest * WIDE, WIDE), WIDE)],
            xa.at[q, ten],
            a2a_s.at[i],
            a2a_r.at[i],
            (dest * 2 + core, ten),
        )

    def a2a_start(i, carry):
        a2a_copy(i).start()
        return carry

    lax.fori_loop(1, NQ, a2a_start, 0)

    loads[4].wait()
    loads[5].wait()
    tapst[...] = taps_v[...].astype(F32).T

    halo_delta.wait_recv()
    keep_d = jnp.where(con == 31, 0.0, 1.0).astype(F32)
    dext[pl.ds(ROWS, ROWS), :] = halo_d[...].astype(F32) * keep_d
    for r in range(8):
        d8[r, pl.ds(0, 248), :] = dext[pl.ds(r, 248), :]

    def lanes(l):
        return pl.ds(pl.multiple_of(l * 128, 128), 128)

    def back_tile(l, carry):
        cols = lanes(l)

        acc = gain_v[:, cols] * d8[0, pl.ds(0, ROWS), cols]
        for r in range(8):
            for a in range(16):
                acc = acc + tapst[pl.ds(8 * a + r, 1), cols] * d8[r, pl.ds(8 * a, ROWS), cols]
        back[:, cols] = acc
        return carry

    lax.fori_loop(0, 4, back_tile, 0)

    backs = back[...]
    kgv[...] = (backs * vv[...].astype(F32)).astype(BF16)
    ga[q] = (backs * kv[...].astype(F32)).astype(BF16)

    def slot(zz, rel):
        return (zz % NZ) * 2 + (yl + rel) % 2

    def b_copy(index, where, device):
        return remote(ga.at[where], ga.at[where], b_s.at[index], b_r.at[index], (device, ten))

    up, down = at(z + 1, yl, core), at(z + 7, yl, core)

    def right(d, rel):
        return b_copy(1 + (d - 1) * 4 + rel, slot(z + 9 - d, rel), up)

    def left(d, rel):
        return b_copy(1 + (d - 1) * 4 + 2 + rel, slot(z + d - 1, rel), down)

    def arrived_right(d, rel):
        b_copy(1 + (d - 1) * 4 + rel, slot(z + 8 - d, rel), up).wait_recv()

    def arrived_left(d, rel):
        b_copy(1 + (d - 1) * 4 + 2 + rel, slot(z + d, rel), down).wait_recv()

    right(1, 0).start()
    left(1, 0).start()
    across = b_copy(0, slot(z, 0), at(z, yl + 1, core))
    across.start()

    out_copies = [
        pltpu.make_async_copy(kgv, kg_hbm, out_sems.at[0]),
        pltpu.make_async_copy(ga.at[q], vg_hbm, out_sems.at[1]),
    ]
    for copy in out_copies:
        copy.start()

    own_x.wait()

    def a2a_wait(i, carry):
        source = ((z + NZ - i // 2) % NZ) * 2 + (yl + i % 2) % 2
        remote(xa.at[source, ten], xa.at[source, ten], a2a_s.at[i], a2a_r.at[i], (source * 2 + core, ten)).wait_recv()
        return carry

    lax.fori_loop(1, NQ, a2a_wait, 0)

    def ag_copy(index, part, half, device):
        ref = xa.at[:, part] if half is None else xa.at[pl.ds(8 * half, 8), part]
        return remote(ref, ref, ag_s.at[index], ag_r.at[index], (con, device))

    x_up, x_down = ten_at(yh, x + 1), ten_at(yh, x + 3)
    other = ten_at(yh + 1, x)
    ag_y = ag_copy(0, ten, None, other)
    ag_y.start()
    ag_copy(1, ten, None, x_up).start()
    ag_copy(2, ten, None, x_down).start()

    loads[6].wait()

    def c_copy(i, chunk):
        cols = pl.ds(chunk * CCOLS, CCOLS)
        index = i * CHUNKS + chunk
        return remote(
            tpart.at[(ten + i) % NT, :, cols], trecv.at[i, :, cols], c_s.at[index], c_r.at[index], (con, (ten + i) % NT)
        )

    def terms(chunk):
        def part(n, carry):
            cols = pl.ds(pl.multiple_of(chunk * CCOLS + n * 512, 512), 512)
            product = lax.dot_general(ga[q], w_v[cols, :], (((1,), (1,)), ((), ())), preferred_element_type=F32)
            tpart[:, :, cols] = product.astype(BF16).reshape(NT, SUB, 512)
            return carry

        lax.fori_loop(0, CCOLS // 512, part, 0)

        def send(i, carry):
            c_copy(i, chunk).start()
            return carry

        lax.fori_loop(1, NT, send, 0)

    terms(0)
    terms(1)
    across.wait_recv()
    right(1, 1).start()
    left(1, 1).start()
    terms(2)
    terms(3)

    def filter_tile(l, carry):
        cols = lanes(l)

        for r in range(8):
            for a in range(16):
                product = iext[pl.ds(ROWS, ROWS), cols] * d8[r, pl.ds(8 * a, ROWS), cols]
                fpart[pl.ds(8 * a + r, 1), cols] = jnp.sum(product, axis=0, keepdims=True)
        return carry

    def forward(d, rel):
        arrived_right(d, rel)
        if d < 3 or rel == 0:
            right(d + 1, rel).start()
        arrived_left(d, rel)
        if d < 3 or rel == 1:
            left(d + 1, rel).start()

    lax.fori_loop(0, 2, filter_tile, 0)
    forward(1, 0)
    ag_y.wait_recv()
    ag_copy(3, other, None, x_up).start()
    ag_copy(4, other, None, x_down).start()
    lax.fori_loop(2, 4, filter_tile, 0)
    forward(1, 1)

    half = CH // 2
    mine = pl.ds(pl.multiple_of(core * half, half), half)
    theirs = pl.ds(pl.multiple_of((1 - core) * half, half), half)
    partner = (at(z, yl, core + 1), ten)
    f_core = remote(fpart.at[:, theirs], fcore, core_s.at[0], core_r.at[0], partner)
    f_core.start()

    ag_copy(1, x_down, None, x_up).wait_recv()
    ag_copy(5, x_down, 0, x_up).start()
    ag_copy(2, x_up, None, x_down).wait_recv()
    ag_copy(6, x_up, 1, x_down).start()

    halo_inner.wait_recv()
    keep_i = jnp.where(con == 0, 0.0, 1.0).astype(F32)
    iext[pl.ds(0, ROWS), :] = halo_i[...].astype(F32) * keep_i
    e8[0] = iext[...]
    for r in range(1, 8):
        e8[r, pl.ds(0, 248), :] = iext[pl.ds(r, 248), :]

    f_core.wait_recv()
    fsum[...] = fpart[:, mine] + fcore[...]

    def rs_copy(i):
        dest = ((z + i // 2) % NZ) * 2 + (yl + i % 2) % 2
        return remote(
            fsum.at[pl.ds(pl.multiple_of(dest * 8, 8), 8), :], frs.at[i], rs_s.at[i], rs_r.at[i], (dest * 2 + core, ten)
        )

    def rs_start(i, carry):
        rs_copy(i).start()
        return carry

    lax.fori_loop(1, NQ, rs_start, 0)

    def mixed_tile(l, carry):
        cols = lanes(l)
        acc = iext[pl.ds(ROWS, ROWS), cols] * gain_v[:, cols]
        for r in range(8):
            for b in range(17):
                if 0 <= TAPS - 8 * b - r < TAPS:
                    acc = acc + tapst[pl.ds(TAPS - 8 * b - r, 1), cols] * e8[r, pl.ds(8 * b, ROWS), cols]
        qgv[:, cols] = (gv[:, cols].astype(F32) * acc).astype(BF16)
        return carry

    lax.fori_loop(0, 2, mixed_tile, 0)
    forward(2, 0)
    lax.fori_loop(2, 4, mixed_tile, 0)
    forward(2, 1)
    copy = pltpu.make_async_copy(qgv, qg_hbm, out_sems.at[2])
    copy.start()
    out_copies.append(copy)

    def rs_wait(i, carry):
        rs_copy(i).wait_recv()
        return carry

    lax.fori_loop(1, NQ, rs_wait, 0)
    total = fsum[pl.ds(pl.multiple_of(q * 8, 8), 8), :]
    for i in range(1, NQ):
        total = total + frs[i]
    my_rows = pl.ds(pl.multiple_of(q * 8, 8), 8)
    ffull[my_rows, mine] = total

    def fa_copy(i, source):
        dest = ((z + i // 2) % NZ) * 2 + (yl + i % 2) % 2
        ref = ffull.at[pl.ds(pl.multiple_of(source * 8, 8), 8), mine]
        return remote(ref, ref, fa_s.at[i], fa_r.at[i], (dest * 2 + core, ten))

    def fa_start(i, carry):
        fa_copy(i, q).start()
        return carry

    lax.fori_loop(1, NQ, fa_start, 0)

    other_down, other_up = ten_at(yh + 1, x + 3), ten_at(yh + 1, x + 1)
    ag_copy(3, other_down, None, x_up).wait_recv()
    ag_copy(7, other_down, 0, x_up).start()
    ag_copy(4, other_up, None, x_down).wait_recv()
    ag_copy(8, other_up, 1, x_down).start()

    forward(3, 0)
    forward(3, 1)

    def fa_wait(i, carry):
        source = ((z + NZ - i // 2) % NZ) * 2 + (yl + i % 2) % 2
        fa_copy(i, source).wait_recv()
        return carry

    lax.fori_loop(1, NQ, fa_wait, 0)
    f_back = remote(ffull.at[:, mine], ffull.at[:, mine], core_s.at[1], core_r.at[1], partner)
    f_back.start()

    arrived_right(4, 0)
    arrived_left(4, 1)

    def product(part, first):
        def rows(m, carry):
            cols = pl.ds(pl.multiple_of(m * 256, 256), 256)
            lhs = xa[:, part, :, cols].reshape(NQ * SUB, 256)
            rhs = ga[:, pl.ds(pl.multiple_of(part * SUB, SUB), SUB), :].reshape(NQ * SUB, CH)
            new = lax.dot_general(lhs, rhs, (((0,), (0,)), ((), ())), preferred_element_type=F32)
            if first:
                wacc[cols, :] = new
            else:
                wacc[cols, :] += new
            return carry

        lax.fori_loop(0, 2, rows, 0)

    product(ten, True)
    product(x_up, False)
    product(x_down, False)
    product(other, False)
    product(other_up, False)
    product(other_down, False)

    f_back_wait = remote(ffull.at[:, theirs], ffull.at[:, theirs], core_s.at[1], core_r.at[1], partner)
    f_back_wait.wait_recv()
    fgt[...] = ffull[...].T
    sgv[...] = ffull[pl.ds(0, 1), :]
    for copy in (
        pltpu.make_async_copy(fgt, fg_hbm, out_sems.at[3]),
        pltpu.make_async_copy(sgv, sg_hbm, out_sems.at[4]),
    ):
        copy.start()
        out_copies.append(copy)

    far, other_far = ten_at(yh, x + 2), ten_at(yh + 1, x + 2)
    ag_copy(5, far, 0, x_up).wait_recv()
    ag_copy(6, far, 1, x_down).wait_recv()
    product(far, False)
    ag_copy(7, other_far, 0, x_up).wait_recv()
    ag_copy(8, other_far, 1, x_down).wait_recv()
    product(other_far, False)
    own_rows = pl.ds(pl.multiple_of(core * 256, 256), 256)
    partner_rows = pl.ds(pl.multiple_of((1 - core) * 256, 256), 256)
    w_core = remote(wacc.at[partner_rows, :], wrecv, core_s.at[2], core_r.at[2], partner)
    w_core.start()

    for chunk in range(CHUNKS):
        for i in range(1, NT):
            c_copy(i, chunk).wait_recv()
        cols = pl.ds(chunk * CCOLS, CCOLS)
        acc = tpart[ten, :, cols].astype(F32)
        for i in range(1, NT):
            acc = acc + trecv[i, :, cols].astype(F32)
        ig[:, cols] = acc.astype(BF16)
    copy = pltpu.make_async_copy(ig, ig_hbm, out_sems.at[5])
    copy.start()
    out_copies.append(copy)

    w_core.wait_recv()
    wout[...] = wacc[own_rows, :] + wrecv[...]
    copy = pltpu.make_async_copy(wout, wg_hbm, out_sems.at[6])
    copy.start()
    out_copies.append(copy)

    halo_delta.wait_send()
    halo_inner.wait_send()

    def sent(i, carry):
        a2a_copy(i).wait_send()
        rs_copy(i).wait_send()
        fa_copy(i, q).wait_send()
        return carry

    lax.fori_loop(1, NQ, sent, 0)
    for index in range(9):
        ag_copy(index, ten, None if index < 5 else 0, x_up).wait_send()
    for index in range(15):
        b_copy(index if index < 14 else 16, slot(z, 0), up).wait_send()

    def c_sent(i, carry):
        for chunk in range(CHUNKS):
            c_copy(i, chunk).wait_send()
        return carry

    lax.fori_loop(1, NT, c_sent, 0)
    f_core.wait_send()
    f_back.wait_send()
    w_core.wait_send()
    for copy in out_copies:
        copy.wait()


def local(layer_input, query_stream, key_stream, value_stream, output_grad, filter_taps, skip_gain, value_weight):
    shape = jax.ShapeDtypeStruct
    vm = pltpu.VMEM
    dma = pltpu.SemaphoreType.DMA
    outs = pl.pallas_call(
        kernel,
        out_shape=(
            shape((ROWS, CH), BF16),
            shape((ROWS, CH), BF16),
            shape((ROWS, CH), BF16),
            shape((CH, TAPS), F32),
            shape((1, CH), F32),
            shape((SUB, D), BF16),
            shape((256, CH), F32),
        ),
        in_specs=[pl.BlockSpec(memory_space=pl.ANY)] * 8,
        out_specs=[pl.BlockSpec(memory_space=pl.ANY)] * 7,
        scratch_shapes=[
            vm((ROWS, CH), BF16),
            vm((ROWS, CH), BF16),
            vm((ROWS, CH), BF16),
            vm((ROWS, CH), BF16),
            vm((CH, TAPS), BF16),
            vm((1, CH), F32),
            vm((D, CH), BF16),
            vm((ROWS, CH), BF16),
            vm((ROWS, CH), BF16),
            vm((ROWS, CH), BF16),
            vm((ROWS, CH), BF16),
            vm((TAPS, CH), F32),
            vm((2 * ROWS, CH), F32),
            vm((2 * ROWS, CH), F32),
            vm((8, 2 * ROWS, CH), F32),
            vm((8, 2 * ROWS, CH), F32),
            vm((ROWS, CH), F32),
            vm((ROWS, CH), BF16),
            vm((ROWS, CH), BF16),
            vm((NQ, NT, SUB, WIDE), BF16),
            vm((NQ, ROWS, CH), BF16),
            vm((NT, SUB, D), BF16),
            vm((NT, SUB, D), BF16),
            vm((SUB, D), BF16),
            vm((WIDE, CH), F32),
            vm((256, CH), F32),
            vm((256, CH), F32),
            vm((TAPS, CH), F32),
            vm((TAPS, CH // 2), F32),
            vm((TAPS, CH // 2), F32),
            vm((NQ, 8, CH // 2), F32),
            vm((TAPS, CH), F32),
            vm((CH, TAPS), F32),
            vm((1, CH), F32),
            dma((8,)),
            dma((7,)),
            dma((2,)), dma((2,)),
            dma((NQ,)), dma((NQ,)),
            dma((9,)), dma((9,)),
            dma((17,)), dma((17,)),
            dma((NT * CHUNKS,)), dma((NT * CHUNKS,)),
            dma((3,)), dma((3,)),
            dma((NQ,)), dma((NQ,)),
            dma((NQ,)), dma((NQ,)),
        ],
        compiler_params=pltpu.CompilerParams(
            collective_id=0, has_side_effects=True, vmem_limit_bytes=52 << 20
        ),
        name="hyena_back",
    )(
        layer_input, query_stream, key_stream, value_stream, output_grad, filter_taps,
        skip_gain.reshape(1, CH), value_weight,
    )
    query_grad, key_grad, value_grad, filter_grad, skip_grad, input_grad, weight_grad = outs
    return (query_grad, key_grad, value_grad, filter_grad, skip_grad.reshape(CH), input_grad, weight_grad)


def solution(mesh):
    placed = (
        P(("context", "tensor"), None),
        P("context", "tensor"),
        P("context", "tensor"),
        P("context", "tensor"),
        P("context", "tensor"),
        P("tensor", None),
        P("tensor"),
        P(None, "tensor"),
    )
    return jax.shard_map(
        local,
        mesh=mesh,
        in_specs=placed,
        out_specs=(
            P("context", "tensor"),
            P("context", "tensor"),
            P("context", "tensor"),
            P("tensor", None),
            P("tensor"),
            P(("context", "tensor"), None),
            P("context", "tensor"),
        ),
        check_vma=False,
    )
```

time: 597 us -> 88.9 us (0.15)
  waiting for transfers between devices: 400 us -> 0 us
  matrix products: 87 us -> 0 us
  Pallas kernels: 0 us -> 76 us
  blocking collectives: 55.9 us -> 0 us
  local copies, waits for them, and re-layouts: 29.4 us -> 12 us
  between operations: 14 us -> 0.66 us
  starting transfers between devices: 7.41 us -> 0 us
    psum x1 -> x0, waiting for transfers between devices: 224 us -> none  [local(): filter_grad, skip_grad = lax.psum((taps_local, skip_local), 'context')]
    reduce_scatter x2 -> x0, waiting for transfers between devices: 166 us -> none  [the longest x1 84.3 us: local(): lax.psum_scatter(lax.dot_general(value_grad, value_weight, (((1,), (1,)),...]
    dot_general x7 -> x0, matrix products: 87 us -> none  [the longest x1 31.2 us: local(): jnp.einsum('cts,jts->cj', outer_sums, selector.astype(jnp.float32), preci...]
    pallas_call x0 -> x1, Pallas kernels: none -> 76 us  [local(): pl.pallas_call(kernel, out_shape=(shape((ROWS, CH), BF16), shape((ROWS, C...]
    psum x1 -> x0, blocking collectives: 55.9 us -> none  [local(): filter_grad, skip_grad = lax.psum((taps_local, skip_local), 'context')]
    convert_element_type x1 -> x0, local copies, waits for them, and re-layouts: 24.2 us -> none  [local(): banded = jnp.einsum('cj,jts->cts', filter_taps, selector, preferred_eleme...]
    all_gather x1 -> x0, waiting for transfers between devices: 9.15 us -> none  [local(): gathered = lax.all_gather(layer_input, 'tensor', axis=0, tiled=True)]
    unnamed x19 -> x21, local copies, waits for them, and re-layouts: 4.24 us -> 12 us
  transfers between devices with their start and end apart: 6 -> 0, of which waited for: 4 -> 0; matrix products, arithmetic and copies ran while one was open for 18% -> 0% of each run, Pallas kernels for 0% -> 0%
where the time goes in v1:
time: 88.9 us; the launch traced here: 88.6 us
  Pallas kernels  76 us (85%)
  local copies, waits for them, and re-layouts  12 us (13%)
    pallas_call x1, Pallas kernels, local(): pl.pallas_call(kernel, out_shape=(shape((ROWS, CH), BF16), shape((ROWS, C...  76 us
    unnamed x21, local copies, waits for them, and re-layouts  12 us

profile of v1, /device:TPU:1, one launch (start us, length us, event | category | flops | bytes accessed | tf_op | source)
XLA Modules:
  0.0 88.6 jit_solution(13615071814323989963)
XLA Ops:
  0.6 0.0 copy-start
  0.6 0.9 %copy-done = bf16[16,8192]{1,0:T(8,128)(2,1)S(1)} copy-done((bf16[16,8192]{1,0:T(8,128)(2,1)S(1)}, bf16[16,8192]{1,0:T(8,128)(2,1)}, u32[]{:S(2)}) %copy-start) | copy-done | bytes 262168
  1.6 0.0 copy-start.1
  1.6 0.9 %copy-done.1 = bf16[128,512]{1,0:T(8,128)(2,1)S(1)} copy-done((bf16[128,512]{1,0:T(8,128)(2,1)S(1)}, bf16[128,512]{1,0:T(8,128)(2,1)}, u32[]{:S(2)}) %copy-start.1) | copy-done | bytes 131096
  2.5 0.0 copy-start.2
  2.5 0.9 %copy-done.2 = bf16[128,512]{1,0:T(8,128)(2,1)S(1)} copy-done((bf16[128,512]{1,0:T(8,128)(2,1)S(1)}, bf16[128,512]{1,0:T(8,128)(2,1)}, u32[]{:S(2)}) %copy-start.2) | copy-done | bytes 131096
  3.4 0.0 copy-start.3
  3.4 0.9 %copy-done.3 = bf16[128,512]{1,0:T(8,128)(2,1)S(1)} copy-done((bf16[128,512]{1,0:T(8,128)(2,1)S(1)}, bf16[128,512]{1,0:T(8,128)(2,1)}, u32[]{:S(2)}) %copy-start.3) | copy-done | bytes 131096
  4.3 0.0 copy-start.4
  4.3 0.9 %copy-done.4 = bf16[128,512]{1,0:T(8,128)(2,1)S(1)} copy-done((bf16[128,512]{1,0:T(8,128)(2,1)S(1)}, bf16[128,512]{1,0:T(8,128)(2,1)}, u32[]{:S(2)}) %copy-start.4) | copy-done | bytes 131096
  5.2 0.0 copy-start.5
  5.2 0.9 %copy-done.5 = bf16[512,128]{1,0:T(8,128)(2,1)S(1)} copy-done((bf16[512,128]{1,0:T(8,128)(2,1)S(1)}, bf16[512,128]{1,0:T(8,128)(2,1)}, u32[]{:S(2)}) %copy-start.5) | copy-done | bytes 131096
  6.1 0.0 copy-start.6
  6.1 0.7 copy-done.6
  6.8 76.0 %hyena_back.1 = (bf16[128,512]{1,0:T(8,128)(2,1)S(1)}, bf16[128,512]{1,0:T(8,128)(2,1)S(1)}, bf16[128,512]{1,0:T(8,128)(2,1)S(1)}, f32[512,128]{1,0:T(8,128)S(1)...) custom-call(bf16[16,8192]{1,0:T(8,128)(2,1)S(1)} %copy-done, ...), custom_call_target="tpu_custom_call" | custom-call | tf_op jit(solution)/shard_map/hyena_back/pallas_call | solution.py:450
  82.8 0.7 copy.22
  83.5 0.7 copy.23
  84.1 0.7 copy.24
  84.8 0.7 copy.25
  85.5 0.6 copy.26
  86.1 0.7 copy.27
  86.8 1.9 %copy.28 = f32[256,512]{1,0:T(8,128)} copy(f32[256,512]{1,0:T(8,128)} %get-tuple-element.34) | data formatting | bytes 1048576
Async XLA Ops:
  0.6 1.0 %copy-start = (bf16[16,8192]{1,0:T(8,128)(2,1)S(1)}, bf16[16,8192]{1,0:T(8,128)(2,1)}, u32[]{:S(2)}) copy-start(bf16[16,8192]{1,0:T(8,128)(2,1)} %x_hbm.1) | copy-start | bytes 786436
  1.6 0.9 %copy-start.1 = (bf16[128,512]{1,0:T(8,128)(2,1)S(1)}, bf16[128,512]{1,0:T(8,128)(2,1)}, u32[]{:S(2)}) copy-start(bf16[128,512]{1,0:T(8,128)(2,1)} %q_hbm.1) | copy-start | bytes 393220
  2.5 0.9 %copy-start.2 = (bf16[128,512]{1,0:T(8,128)(2,1)S(1)}, bf16[128,512]{1,0:T(8,128)(2,1)}, u32[]{:S(2)}) copy-start(bf16[128,512]{1,0:T(8,128)(2,1)} %k_hbm.1) | copy-start | bytes 393220
  3.4 0.9 %copy-start.3 = (bf16[128,512]{1,0:T(8,128)(2,1)S(1)}, bf16[128,512]{1,0:T(8,128)(2,1)}, u32[]{:S(2)}) copy-start(bf16[128,512]{1,0:T(8,128)(2,1)} %v_hbm.1) | copy-start | bytes 393220
  4.3 0.9 %copy-start.4 = (bf16[128,512]{1,0:T(8,128)(2,1)S(1)}, bf16[128,512]{1,0:T(8,128)(2,1)}, u32[]{:S(2)}) copy-start(bf16[128,512]{1,0:T(8,128)(2,1)} %g_hbm.1) | copy-start | bytes 393220
  5.2 0.9 %copy-start.5 = (bf16[512,128]{1,0:T(8,128)(2,1)S(1)}, bf16[512,128]{1,0:T(8,128)(2,1)}, u32[]{:S(2)}) copy-start(bf16[512,128]{1,0:T(8,128)(2,1)} %taps_hbm.1) | copy-start | bytes 393220
  6.1 0.7 copy-start.6

commit v2 on v1

v2 whole, which is shorter than its diff:
```python
import jax
import jax.numpy as jnp
from jax import lax
from jax.experimental import pallas as pl
from jax.experimental.pallas import tpu as pltpu
from jax.sharding import PartitionSpec as P

MESH = pl.DeviceIdType.MESH
BF16 = jnp.bfloat16
F32 = jnp.float32

NZ, NYL, NCORE, NYH, NX = 8, 2, 2, 2, 4
NQ = NZ * NYL
NT = NYH * NX
TAPS = 128
ROWS = 128
CH = 512
SUB = 16
D = 8192
WIDE = D // NQ
CHUNKS = 4
CCOLS = D // CHUNKS
X_FIRST = (0,)
ORDER = (0, 1, 7, 2, 6, 3, 5, 4)
VMEM_LIMIT = 63 << 20
PIECES = (1, 1, 1, 2, 1, 1, 4)


def kernel(
    x_hbm, q_hbm, k_hbm, v_hbm, g_hbm, taps_hbm, gain_hbm, w_hbm,
    qg_hbm, kg_hbm, vg_hbm, fg_hbm, sg_hbm, ig_hbm, wg_hbm,
    qv, kv, vv, gv, taps_v, gain_v, x_v, w_v,
    inner, delta, halo_d, halo_i, tapst, dext, iext, d8, e8, back, mix,
    qgv, kgv, xa, ga, tpart, yr, sums, from_left, from_right, left_sum, right_sum, ysend, isum, ig, wacc, wrecv, wout,
    fpart, fcore, fsum, frs, ffull, fgt, sgv,
    in_sems, out_sems, halo_s, halo_r, a2a_s, a2a_r, ag_s, ag_r, b_s, b_r, c_s, c_r,
    core_s, core_r, rs_s, rs_r, fa_s, fa_r,
):
    con = lax.axis_index("context")
    ten = lax.axis_index("tensor")
    z, yl, core = con // 4, (con // 2) % 2, con % 2
    yh, x = ten // 4, ten % 4
    q = con // 2

    def at(zz, yy, cc):
        return (zz % NZ) * 4 + (yy % 2) * 2 + cc % 2

    def ten_at(hh, xx):
        return (hh % 2) * 4 + xx % 4

    def remote(src, dst, ss, rs, device):
        return pltpu.make_async_remote_copy(
            src_ref=src, dst_ref=dst, send_sem=ss, recv_sem=rs, device_id=device, device_id_type=MESH
        )

    loads = [
        pltpu.make_async_copy(src, dst, in_sems.at[i])
        for i, (src, dst) in enumerate(
            [(k_hbm, kv), (v_hbm, vv), (g_hbm, gv), (q_hbm, qv), (taps_hbm, taps_v), (gain_hbm, gain_v), (x_hbm, x_v), (w_hbm, w_v)]
        )
    ]
    for copy in loads:
        copy.start()

    barrier = pltpu.get_barrier_semaphore()
    above = (con + 1) % 32
    below = (con + 31) % 32

    def greet(device):
        pl.semaphore_signal(barrier, inc=1, device_id=device, device_id_type=MESH)

    greet((above, ten))
    greet((below, ten))
    greet((at(z, yl, core + 1), ten))

    def greet_q(i, carry):
        greet((at(z + i // 2, yl + i % 2, core), ten))
        return carry

    lax.fori_loop(1, NQ, greet_q, 0)

    def greet_t(i, carry):
        greet((con, (ten + i) % NT))
        return carry

    lax.fori_loop(1, NT, greet_t, 0)

    loads[0].wait()
    loads[1].wait()
    loads[2].wait()
    loads[3].wait()
    inner[...] = (kv[...].astype(F32) * vv[...].astype(F32)).astype(BF16)
    delta[...] = (gv[...].astype(F32) * qv[...].astype(F32)).astype(BF16)
    pl.semaphore_wait(barrier, 3 + (NQ - 1) + (NT - 1))

    halo_delta = remote(delta, halo_d, halo_s.at[0], halo_r.at[0], (below, ten))
    halo_inner = remote(inner, halo_i, halo_s.at[1], halo_r.at[1], (above, ten))
    halo_delta.start()

    own_x = pltpu.make_async_copy(
        x_v.at[:, pl.ds(pl.multiple_of(q * WIDE, WIDE), WIDE)], xa.at[0, 0], in_sems.at[8]
    )
    loads[6].wait()
    own_x.start()

    def a2a_copy(slot):
        dest = ((z + ORDER[slot // 2]) % NZ) * 2 + (yl + slot % 2) % 2
        return remote(
            x_v.at[:, pl.ds(pl.multiple_of(dest * WIDE, WIDE), WIDE)],
            xa.at[slot, 0],
            a2a_s.at[slot],
            a2a_r.at[slot],
            (dest * 2 + core, ten),
        )

    for slot in range(1, NQ):
        a2a_copy(slot).start()
    halo_inner.start()

    dext[pl.ds(0, ROWS), :] = delta[...].astype(F32)
    iext[pl.ds(ROWS, ROWS), :] = inner[...].astype(F32)

    loads[4].wait()
    loads[5].wait()
    tapst[...] = taps_v[...].astype(F32).T

    for r in range(8):
        d8[r, pl.ds(0, 15)] = dext[pl.ds(r, 120), :].reshape(15, 8, CH)

    def lanes(l):
        return pl.ds(pl.multiple_of(l * 128, 128), 128)

    def tap_row(j, cols):
        return jnp.broadcast_to(tapst[pl.ds(j, 1), cols], (8, 128))

    def chain(taps, tiles):
        total = taps[0] * tiles[0]
        for tap, tile in zip(taps[1:], tiles[1:]):
            total = total + tap * tile
        return total

    def back_own(l, carry):
        cols = lanes(l)
        gain = jnp.broadcast_to(gain_v[:, cols], (8, 128))
        for r in range(8):
            tiles = [d8[r, k, :, cols] for k in range(15)]
            taps = [tap_row(8 * a + r, cols) for a in range(15)]
            for i in range(15):
                total = chain(taps[: 15 - i], tiles[i:])
                back[i, :, cols] = total + gain * tiles[i] if r == 0 else back[i, :, cols] + total
        back[15, :, cols] = gain * dext[pl.ds(120, 8), cols]
        return carry

    def back_halo(l, carry):
        cols = lanes(l)
        for r in range(8):
            tiles = [d8[r, 15 + k, :, cols] for k in range(16)]
            taps = [tap_row(8 * a + r, cols) for a in range(16)]
            for i in range(16):
                back[i, :, cols] = back[i, :, cols] + chain(taps[15 - i :], tiles[: i + 1])
        return carry

    lax.fori_loop(0, 4, back_own, 0)

    x_up, x_down = ten_at(yh, x + 1), ten_at(yh, x + 3)
    other = ten_at(yh + 1, x)

    def ag_copy(index, phase, source, target, device):
        slots = pl.ds(8 * phase, 8)
        return remote(xa.at[slots, source], xa.at[slots, target], ag_s.at[index], ag_r.at[index], (con, device))

    def ag_y(phase):
        return ag_copy(phase, phase, 0, 1, other)

    def ag_x(phase, row, way):
        index = 2 + phase * 4 + row * 2 + way
        return ag_copy(index, phase, row, 2 + 2 * row + way, x_down if way else x_up)

    def ag_far(phase, row):
        index = 10 + phase * 2 + row
        return ag_copy(index, phase, 2 + 2 * row + phase, 6 + row, x_down if phase else x_up)

    def ag_own(phase):
        if phase == 0:
            own_x.wait()
        for slot in range(max(1, 8 * phase), 8 * phase + 8):
            a2a_copy(slot).wait_recv()
        ag_y(phase).start()
        ag_x(phase, 0, 0).start()
        ag_x(phase, 0, 1).start()

    def ag_other(phase):
        ag_y(phase).wait_recv()
        ag_x(phase, 1, 0).start()
        ag_x(phase, 1, 1).start()

    def ag_forward(phase, row):
        ag_x(phase, row, phase).wait_recv()
        ag_far(phase, row).start()

    ag_own(0)

    halo_delta.wait_recv()
    keep_d = jnp.where(con == 31, 0.0, 1.0).astype(F32)
    dext[pl.ds(ROWS, ROWS), :] = halo_d[...].astype(F32) * keep_d
    for r in range(8):
        d8[r, pl.ds(15, 16)] = dext[pl.ds(120 + r, ROWS), :].reshape(16, 8, CH)
    lax.fori_loop(0, 4, back_halo, 0)

    backs = back[...].reshape(ROWS, CH)
    ga[0] = (backs * kv[...].astype(F32)).astype(BF16)

    def b_copy(index, source, target, device):
        return remote(ga.at[source], ga.at[target], b_s.at[index], b_r.at[index], (device, ten))

    up, down = at(z + 1, yl, core), at(z + 7, yl, core)

    def slot_of(dz, rel):
        return 2 * ORDER.index(dz % NZ) + rel

    def right(d, rel):
        return b_copy(1 + (d - 1) * 4 + rel, slot_of(d - 1, rel), slot_of(d, rel), up)

    def left(d, rel):
        return b_copy(1 + (d - 1) * 4 + 2 + rel, slot_of(1 - d, rel), slot_of(-d, rel), down)

    def forward(d, rel):
        right(d, rel).wait_recv()
        if d < 3 or rel == 0:
            right(d + 1, rel).start()
        left(d, rel).wait_recv()
        if d < 3 or rel == 1:
            left(d + 1, rel).start()

    right(1, 0).start()
    left(1, 0).start()
    across = b_copy(0, 0, 1, at(z, yl + 1, core))
    across.start()

    ag_own(1)

    loads[7].wait()

    ccols = [pl.ds(chunk * CCOLS, CCOLS) for chunk in range(CHUNKS)]
    first_half = [pl.ds(chunk * CCOLS, CCOLS // 2) for chunk in range(CHUNKS)]
    second_half = [pl.ds(chunk * CCOLS + CCOLS // 2, CCOLS // 2) for chunk in range(CHUNKS)]
    lo, hi = pl.ds(0, CCOLS // 2), pl.ds(CCOLS // 2, CCOLS // 2)
    hops = [(x + dx) % 4 for dx in range(4)]

    def c_remote(chunk, kind, src, dst, device):
        index = chunk * 8 + kind
        return remote(src, dst, c_s.at[index], c_r.at[index], (con, device))

    def y_copy(chunk):
        return c_remote(chunk, 0, tpart.at[1 - yh, :, :, ccols[chunk]], yr.at[:, :, ccols[chunk]], other)

    def x_refs(chunk, dx, part):
        if chunk in X_FIRST:
            return tpart.at[:, hops[dx], :, part[chunk]]
        return sums.at[pl.ds(0, 1), dx, :, part[chunk]]

    def groups(chunk):
        return pl.ds(0, 2) if chunk in X_FIRST else pl.ds(0, 1)

    def x_copy(chunk, kind):
        g = groups(chunk)
        src, dst, device = (
            (x_refs(chunk, 2, first_half), from_left.at[chunk, g, :, lo], x_up),
            (x_refs(chunk, 2, second_half), from_right.at[chunk, g, :, hi], x_down),
            (x_refs(chunk, 1, second_half), left_sum.at[chunk, g, :, hi], x_up),
            (x_refs(chunk, 3, first_half), right_sum.at[chunk, g, :, lo], x_down),
            (sums.at[g, 1, :, first_half[chunk]], left_sum.at[chunk, g, :, lo], x_up),
            (sums.at[g, 3, :, second_half[chunk]], right_sum.at[chunk, g, :, hi], x_down),
        )[kind]
        return c_remote(chunk, 1 + kind, src, dst, device)

    def yx_copy(chunk):
        return c_remote(chunk, 7, ysend.at[:, ccols[chunk]], yr.at[0, :, ccols[chunk]], other)

    def f32(ref, *index):
        return ref[index].astype(F32)

    def terms(chunk):
        def part(n, carry):
            cols = pl.ds(pl.multiple_of(chunk * CCOLS + n * 512, 512), 512)
            product = lax.dot_general(ga[0], w_v[cols, :], (((1,), (1,)), ((), ())), preferred_element_type=F32)
            tpart[:, :, :, cols] = product.astype(BF16).reshape(NYH, NX, SUB, 512)
            return carry

        lax.fori_loop(0, CCOLS // 512, part, 0)
        if chunk in X_FIRST:
            for kind in range(4):
                x_copy(chunk, kind).start()
        else:
            y_copy(chunk).start()

    def c_sum_y(chunk):
        y_copy(chunk).wait_recv()
        for dx in (2, 1, 3):
            total = f32(tpart, yh, hops[dx], slice(None), ccols[chunk]) + f32(yr, hops[dx], slice(None), ccols[chunk])
            sums[0, dx, :, ccols[chunk]] = total.astype(BF16)
        for kind in range(4):
            x_copy(chunk, kind).start()

    def c_pass_on(chunk):
        g = groups(chunk)
        for kind, dx, part, here, arrived in ((0, 1, first_half, lo, from_left), (1, 3, second_half, hi, from_right)):
            x_copy(chunk, kind).wait_recv()
            mine = x_refs(chunk, dx, part)[...].astype(F32)
            sums[g, dx, :, part[chunk]] = (mine + f32(arrived, chunk, g, slice(None), here)).astype(BF16)
            x_copy(chunk, kind + 4).start()

    def c_wait_x(chunk):
        for kind in range(2, 6):
            x_copy(chunk, kind).wait_recv()

    def c_turn_y(chunk):
        c_wait_x(chunk)
        cols = ccols[chunk]

        def total(h):
            return f32(tpart, h, x, slice(None), cols) + f32(left_sum, chunk, h) + f32(right_sum, chunk, h)

        ysend[:, cols] = total(1 - yh).astype(BF16)
        yx_copy(chunk).start()
        isum[:, cols] = total(yh)

    def c_end(chunk):
        cols = ccols[chunk]
        if chunk in X_FIRST:
            yx_copy(chunk).wait_recv()
            ig[:, cols] = (isum[:, cols] + f32(yr, 0, slice(None), cols)).astype(BF16)
        else:
            c_wait_x(chunk)
            total = f32(tpart, yh, x, slice(None), cols) + f32(yr, x, slice(None), cols)
            ig[:, cols] = (total + f32(left_sum, chunk, 0) + f32(right_sum, chunk, 0)).astype(BF16)

    def c_sent(chunk):
        for kind in range(6):
            x_copy(chunk, kind).wait_send()
        (yx_copy if chunk in X_FIRST else y_copy)(chunk).wait_send()

    def filter_tile(l, carry):
        cols = lanes(l)
        rows = [iext[pl.ds(ROWS + 8 * i, 8), cols] for i in range(16)]
        for r in range(8):
            tiles = [d8[r, k, :, cols] for k in range(31)]
            for a in range(16):
                total = rows[0] * tiles[a]
                for i in range(1, 16):
                    total = total + rows[i] * tiles[i + a]
                fpart[pl.ds(8 * a + r, 1), cols] = jnp.sum(total, axis=0, keepdims=True)
        return carry

    terms(0)
    ag_other(0)
    terms(1)
    forward(1, 0)
    across.wait_recv()
    right(1, 1).start()
    left(1, 1).start()
    ag_forward(0, 0)
    lax.fori_loop(0, 4, filter_tile, 0)

    half = CH // 2
    mine = pl.ds(pl.multiple_of(core * half, half), half)
    theirs = pl.ds(pl.multiple_of((1 - core) * half, half), half)
    partner = (at(z, yl, core + 1), ten)
    f_core = remote(fpart.at[:, theirs], fcore, core_s.at[0], core_r.at[0], partner)
    f_core.start()
    ag_other(1)
    forward(2, 0)
    terms(2)
    c_pass_on(0)
    ag_forward(1, 0)
    ag_forward(0, 1)
    forward(1, 1)
    terms(3)

    f_core.wait_recv()
    fsum[...] = fpart[:, mine] + fcore[...]

    def q_of(i, way):
        return ((z + NZ + way * (i // 2)) % NZ) * 2 + (yl + i % 2) % 2

    def rs_copy(i):
        dest = q_of(i, 1)
        return remote(
            fsum.at[pl.ds(pl.multiple_of(dest * 8, 8), 8), :], frs.at[i], rs_s.at[i], rs_r.at[i], (dest * 2 + core, ten)
        )

    def rs_start(i, carry):
        rs_copy(i).start()
        return carry

    lax.fori_loop(1, NQ, rs_start, 0)

    kgv[...] = (back[...].reshape(ROWS, CH) * vv[...].astype(F32)).astype(BF16)
    out_copies = [
        pltpu.make_async_copy(kgv, kg_hbm, out_sems.at[0]),
        pltpu.make_async_copy(ga.at[0], vg_hbm, out_sems.at[1]),
    ]
    for copy in out_copies:
        copy.start()


    halo_inner.wait_recv()
    keep_i = jnp.where(con == 0, 0.0, 1.0).astype(F32)
    iext[pl.ds(0, ROWS), :] = halo_i[...].astype(F32) * keep_i
    e8[0] = iext[...].reshape(32, 8, CH)
    for r in range(1, 8):
        e8[r, pl.ds(0, 31)] = iext[pl.ds(r, 248), :].reshape(31, 8, CH)

    def mixed_tile(l, carry):
        cols = lanes(l)
        gain = jnp.broadcast_to(gain_v[:, cols], (8, 128))
        for r in range(8):
            skip = 1 if r == 0 else 0
            taps = [tap_row(TAPS - 8 * (b + skip) - r, cols) for b in range(16)]
            for start in (0, 8):
                tiles = [e8[r, start + k + skip, :, cols] for k in range(23)]
                for i in range(8):
                    total = chain(taps, tiles[i : i + 16])
                    at_i = (start + i, slice(None), cols)
                    mix[at_i] = total + gain * tiles[i + 15] if r == 0 else mix[at_i] + total
        mixed = mix[:, :, cols].reshape(ROWS, 128)
        qgv[:, cols] = (gv[:, cols].astype(F32) * mixed).astype(BF16)
        return carry

    c_sum_y(1)
    forward(3, 0)
    lax.fori_loop(0, 2, mixed_tile, 0)
    ag_forward(1, 1)
    forward(2, 1)
    lax.fori_loop(2, 4, mixed_tile, 0)
    copy = pltpu.make_async_copy(qgv, qg_hbm, out_sems.at[2])
    copy.start()
    out_copies.append(copy)

    far, other_far = ten_at(yh, x + 2), ten_at(yh + 1, x + 2)
    sources = (ten, other, x_down, x_up, ten_at(yh + 1, x + 3), ten_at(yh + 1, x + 1), far, other_far)

    def product(phase, pair, m):
        slots = pl.ds(8 * phase, 8)
        cols = pl.ds(pl.multiple_of(m * 256, 256), 256)
        lhs = xa[slots, pl.ds(2 * pair, 2), :, cols].reshape(256, 256)

        def token_rows(part):
            return ga[slots, pl.ds(pl.multiple_of(part * SUB, SUB), SUB), :]

        rhs = jnp.stack([token_rows(sources[2 * pair]), token_rows(sources[2 * pair + 1])], axis=1).reshape(256, CH)
        new = lax.dot_general(lhs, rhs, (((0,), (0,)), ((), ())), preferred_element_type=F32)
        if phase == 0 and pair == 0:
            wacc[cols, :] = new
        else:
            wacc[cols, :] += new

    if 0 in X_FIRST:
        c_turn_y(0)
    c_pass_on(1)
    c_sum_y(2)
    forward(3, 1)

    def rs_wait(i, carry):
        rs_copy(i).wait_recv()
        return carry

    lax.fori_loop(1, NQ, rs_wait, 0)
    total = fsum[pl.ds(pl.multiple_of(q * 8, 8), 8), :]
    for i in range(1, NQ):
        total = total + frs[i]
    my_rows = pl.ds(pl.multiple_of(q * 8, 8), 8)
    ffull[my_rows, mine] = total

    def fa_copy(i, source):
        ref = ffull.at[pl.ds(pl.multiple_of(source * 8, 8), 8), mine]
        return remote(ref, ref, fa_s.at[i], fa_r.at[i], (q_of(i, 1) * 2 + core, ten))

    def fa_start(i, carry):
        fa_copy(i, q).start()
        return carry

    lax.fori_loop(1, NQ, fa_start, 0)

    product(0, 0, 0)
    product(0, 0, 1)
    ag_x(0, 0, 1).wait_recv()
    product(0, 1, 0)
    product(0, 1, 1)
    ag_x(0, 1, 1).wait_recv()
    product(0, 2, 0)
    product(0, 2, 1)
    c_pass_on(2)
    c_sum_y(3)
    right(4, 0).wait_recv()
    left(4, 1).wait_recv()
    ag_far(0, 0).wait_recv()
    ag_far(0, 1).wait_recv()
    product(0, 3, 0)
    product(0, 3, 1)
    c_end(0)
    c_end(1)
    c_end(2)
    c_pass_on(3)

    def fa_wait(i, carry):
        fa_copy(i, q_of(i, -1)).wait_recv()
        return carry

    lax.fori_loop(1, NQ, fa_wait, 0)
    f_back = remote(ffull.at[:, mine], ffull.at[:, mine], core_s.at[1], core_r.at[1], partner)
    f_back.start()
    product(1, 0, 0)
    product(1, 0, 1)
    ag_x(1, 0, 0).wait_recv()
    product(1, 1, 0)
    product(1, 1, 1)
    ag_x(1, 1, 0).wait_recv()
    product(1, 2, 0)
    product(1, 2, 1)
    ag_far(1, 0).wait_recv()
    ag_far(1, 1).wait_recv()
    partner_rows = pl.ds(pl.multiple_of((1 - core) * 256, 256), 256)
    product(1, 3, 1 - core)
    w_core = remote(wacc.at[partner_rows, :], wrecv, core_s.at[2], core_r.at[2], partner)
    w_core.start()
    product(1, 3, core)

    f_back_wait = remote(ffull.at[:, theirs], ffull.at[:, theirs], core_s.at[1], core_r.at[1], partner)
    f_back_wait.wait_recv()
    fgt[...] = ffull[...].T
    sgv[...] = ffull[pl.ds(0, 1), :]
    for copy in (
        pltpu.make_async_copy(fgt, fg_hbm, out_sems.at[3]),
        pltpu.make_async_copy(sgv, sg_hbm, out_sems.at[4]),
    ):
        copy.start()
        out_copies.append(copy)

    c_end(3)
    copy = pltpu.make_async_copy(ig, ig_hbm, out_sems.at[5])
    copy.start()
    out_copies.append(copy)

    w_core.wait_recv()
    for n in range(4):
        rows = pl.ds(64 * n, 64)
        wout[rows, :] = wacc[pl.ds(pl.multiple_of(core * 256 + 64 * n, 64), 64), :] + wrecv[rows, :]
        copy = pltpu.make_async_copy(wout.at[rows, :], wg_hbm.at[rows, :], out_sems.at[6 + n])
        copy.start()
        out_copies.append(copy)

    halo_delta.wait_send()
    halo_inner.wait_send()

    def sent(i, carry):
        rs_copy(i).wait_send()
        fa_copy(i, q).wait_send()
        return carry

    lax.fori_loop(1, NQ, sent, 0)
    for slot in range(1, NQ):
        a2a_copy(slot).wait_send()
    for phase in range(2):
        ag_y(phase).wait_send()
        for row in range(2):
            ag_x(phase, row, 0).wait_send()
            ag_x(phase, row, 1).wait_send()
            ag_far(phase, row).wait_send()
    across.wait_send()
    for rel in range(2):
        for d in range(1, 4):
            right(d, rel).wait_send()
            left(d, rel).wait_send()
    right(4, 0).wait_send()
    left(4, 1).wait_send()
    for chunk in range(CHUNKS):
        c_sent(chunk)
    f_core.wait_send()
    f_back.wait_send()
    w_core.wait_send()
    for copy in out_copies:
        copy.wait()


def finish(*refs):
    ins, outs, held, (in_sems, out_sems) = refs[:7], refs[7:14], refs[14:21], refs[21:]
    reads, writes = [], []
    for i, pieces in enumerate(PIECES):
        rows = ins[i].shape[0] // pieces
        for n in range(pieces):
            part = pl.ds(rows * n, rows)
            at = len(reads)
            reads.append(pltpu.make_async_copy(ins[i].at[part, :], held[i].at[part, :], in_sems.at[at]))
            writes.append(pltpu.make_async_copy(held[i].at[part, :], outs[i].at[part, :], out_sems.at[at]))
    for read in reads:
        read.start()
    for read, write in zip(reads, writes):
        read.wait()
        write.start()
    for write in writes:
        write.wait()


def local(layer_input, query_stream, key_stream, value_stream, output_grad, filter_taps, skip_gain, value_weight):
    shape = jax.ShapeDtypeStruct
    vm = pltpu.VMEM
    dma = pltpu.SemaphoreType.DMA
    outs = pl.pallas_call(
        kernel,
        out_shape=(
            shape((ROWS, CH), BF16),
            shape((ROWS, CH), BF16),
            shape((ROWS, CH), BF16),
            shape((CH, TAPS), F32),
            shape((1, CH), F32),
            shape((SUB, D), BF16),
            shape((256, CH), F32),
        ),
        in_specs=[pl.BlockSpec(memory_space=pl.ANY)] * 8,
        out_specs=[pl.BlockSpec(memory_space=pl.ANY)] * 7,
        scratch_shapes=[
            vm((ROWS, CH), BF16),
            vm((ROWS, CH), BF16),
            vm((ROWS, CH), BF16),
            vm((ROWS, CH), BF16),
            vm((CH, TAPS), BF16),
            vm((1, CH), F32),
            vm((SUB, D), BF16),
            vm((D, CH), BF16),
            vm((ROWS, CH), BF16),
            vm((ROWS, CH), BF16),
            vm((ROWS, CH), BF16),
            vm((ROWS, CH), BF16),
            vm((TAPS, CH), F32),
            vm((2 * ROWS, CH), F32),
            vm((2 * ROWS, CH), F32),
            vm((8, 32, 8, CH), F32),
            vm((8, 32, 8, CH), F32),
            vm((16, 8, CH), F32),
            vm((16, 8, CH), F32),
            vm((ROWS, CH), BF16),
            vm((ROWS, CH), BF16),
            vm((NQ, NT, SUB, WIDE), BF16),
            vm((NQ, ROWS, CH), BF16),
            vm((NYH, NX, SUB, D), BF16),
            vm((NX, SUB, D), BF16),
            vm((NYH, NX, SUB, D), BF16),
            vm((CHUNKS, NYH, SUB, CCOLS), BF16),
            vm((CHUNKS, NYH, SUB, CCOLS), BF16),
            vm((CHUNKS, NYH, SUB, CCOLS), BF16),
            vm((CHUNKS, NYH, SUB, CCOLS), BF16),
            vm((SUB, D), BF16),
            vm((SUB, D), F32),
            vm((SUB, D), BF16),
            vm((WIDE, CH), F32),
            vm((256, CH), F32),
            vm((256, CH), F32),
            vm((TAPS, CH), F32),
            vm((TAPS, CH // 2), F32),
            vm((TAPS, CH // 2), F32),
            vm((NQ, 8, CH // 2), F32),
            vm((TAPS, CH), F32),
            vm((CH, TAPS), F32),
            vm((1, CH), F32),
            dma((9,)),
            dma((10,)),
            dma((2,)), dma((2,)),
            dma((NQ,)), dma((NQ,)),
            dma((14,)), dma((14,)),
            dma((17,)), dma((17,)),
            dma((8 * CHUNKS,)), dma((8 * CHUNKS,)),
            dma((3,)), dma((3,)),
            dma((NQ,)), dma((NQ,)),
            dma((NQ,)), dma((NQ,)),
        ],
        compiler_params=pltpu.CompilerParams(
            collective_id=0, has_side_effects=True, vmem_limit_bytes=VMEM_LIMIT
        ),
        name="hyena_back",
    )(
        layer_input, query_stream, key_stream, value_stream, output_grad, filter_taps,
        skip_gain.reshape(1, CH), value_weight,
    )
    outs = pl.pallas_call(
        finish,
        out_shape=tuple(shape(out.shape, out.dtype) for out in outs),
        in_specs=[pl.BlockSpec(memory_space=pl.ANY)] * 7,
        out_specs=[pl.BlockSpec(memory_space=pl.ANY)] * 7,
        scratch_shapes=[vm(out.shape, out.dtype) for out in outs] + [dma((sum(PIECES),)), dma((sum(PIECES),))],
        compiler_params=pltpu.CompilerParams(vmem_limit_bytes=VMEM_LIMIT),
        name="finish",
    )(*outs)
    query_grad, key_grad, value_grad, filter_grad, skip_grad, input_grad, weight_grad = outs
    return (query_grad, key_grad, value_grad, filter_grad, skip_grad.reshape(CH), input_grad, weight_grad)


def solution(mesh):
    placed = (
        P(("context", "tensor"), None),
        P("context", "tensor"),
        P("context", "tensor"),
        P("context", "tensor"),
        P("context", "tensor"),
        P("tensor", None),
        P("tensor"),
        P(None, "tensor"),
    )
    return jax.shard_map(
        local,
        mesh=mesh,
        in_specs=placed,
        out_specs=(
            P("context", "tensor"),
            P("context", "tensor"),
            P("context", "tensor"),
            P("tensor", None),
            P("tensor"),
            P(("context", "tensor"), None),
            P("context", "tensor"),
        ),
        check_vma=False,
    )
```

time: 88.9 us -> 62 us (0.70)
  Pallas kernels: 76 us -> 61.3 us
  local copies, waits for them, and re-layouts: 12 us -> 0 us
    pallas_call x1, Pallas kernels: 76 us -> 58.9 us  [local(): pl.pallas_call(kernel, out_shape=(shape((ROWS, CH), BF16), shape((ROWS, C...]
    unnamed x21 -> x0, local copies, waits for them, and re-layouts: 12 us -> none
    pallas_call x0 -> x1, Pallas kernels: none -> 2.32 us  [local(): pl.pallas_call(finish, out_shape=tuple((shape(out.shape, out.dtype) for o...]
where the time goes in v2:
time: 62 us; the launch traced here: 61.9 us
  Pallas kernels  61.3 us (99%)
  between operations  0.64 us (1%)
    pallas_call x1, Pallas kernels, local(): pl.pallas_call(kernel, out_shape=(shape((ROWS, CH), BF16), shape((ROWS, C...  58.9 us
    pallas_call x1, Pallas kernels, local(): pl.pallas_call(finish, out_shape=tuple((shape(out.shape, out.dtype) for o...  2.32 us

profile of v2, /device:TPU:1, one launch (start us, length us, event | category | flops | bytes accessed | tf_op | source)
XLA Modules:
  0.0 61.9 jit_solution(16063928544348075378)
XLA Ops:
  0.6 58.9 %hyena_back.1 = (bf16[128,512]{1,0:T(8,128)(2,1)}, bf16[128,512]{1,0:T(8,128)(2,1)}, bf16[128,512]{1,0:T(8,128)(2,1)}, f32[512,128]{1,0:T(8,128)}, f32[1,512]{1,...) custom-call(bf16[16,8192]{1,0:T(8,128)(2,1)} %x_hbm.1, bf16[128,512]{1,0:T(8,128)(2,1)} %q_hbm.1, ...), custom_call_target="tpu_custom_call" | custom-call | tf_op jit(solution)/shard_map/hyena_back/pallas_call | solution.py:609
  59.6 2.3 %finish.1 = (bf16[128,512]{1,0:T(8,128)(2,1)}, bf16[128,512]{1,0:T(8,128)(2,1)}, bf16[128,512]{1,0:T(8,128)(2,1)}, f32[512,128]{1,0:T(8,128)}, f32[1,512]{1,0:T(...) custom-call(bf16[128,512]{1,0:T(8,128)(2,1)} %get-tuple-element.21.refs_0_, ...), custom_call_target="tpu_custom_call" | custom-call | tf_op jit(solution)/shard_map/finish/pallas_call | solution.py:685

commit v3 on v2

--- a/solution.py
+++ b/solution.py
@@ -59,9 +59,6 @@
             [(k_hbm, kv), (v_hbm, vv), (g_hbm, gv), (q_hbm, qv), (taps_hbm, taps_v), (gain_hbm, gain_v), (x_hbm, x_v), (w_hbm, w_v)]
         )
     ]
-    for copy in loads:
-        copy.start()
-
     barrier = pltpu.get_barrier_semaphore()
     above = (con + 1) % 32
     below = (con + 31) % 32
@@ -69,21 +66,18 @@
     def greet(device):
         pl.semaphore_signal(barrier, inc=1, device_id=device, device_id_type=MESH)
 
+    for dz in (4, 3, 5, 2, 6, 1, 7, 0):
+        for dy in range(2):
+            if (dz, dy) != (0, 0):
+                greet((at(z + dz, yl + dy, core), ten))
+    for i in (6, 2, 5, 7, 4, 1, 3):
+        greet((con, (ten + i) % NT))
     greet((above, ten))
     greet((below, ten))
     greet((at(z, yl, core + 1), ten))
-
-    def greet_q(i, carry):
-        greet((at(z + i // 2, yl + i % 2, core), ten))
-        return carry
-
-    lax.fori_loop(1, NQ, greet_q, 0)
-
-    def greet_t(i, carry):
-        greet((con, (ten + i) % NT))
-        return carry
-
-    lax.fori_loop(1, NT, greet_t, 0)
+    for copy in loads:
+        copy.start()
+
 
     loads[0].wait()
     loads[1].wait()
@@ -108,8 +102,8 @@
         return remote(
             x_v.at[:, pl.ds(pl.multiple_of(dest * WIDE, WIDE), WIDE)],
             xa.at[slot, 0],
-            a2a_s.at[slot],
-            a2a_r.at[slot],
+            a2a_s.at[0],
+            a2a_r.at[slot // 8],
             (dest * 2 + core, ten),
         )
 
@@ -167,7 +161,7 @@
 
     def ag_copy(index, phase, source, target, device):
         slots = pl.ds(8 * phase, 8)
-        return remote(xa.at[slots, source], xa.at[slots, target], ag_s.at[index], ag_r.at[index], (con, device))
+        return remote(xa.at[slots, source], xa.at[slots, target], ag_s.at[0], ag_r.at[index], (con, device))
 
     def ag_y(phase):
         return ag_copy(phase, phase, 0, 1, other)
@@ -183,8 +177,8 @@
     def ag_own(phase):
         if phase == 0:
             own_x.wait()
-        for slot in range(max(1, 8 * phase), 8 * phase + 8):
-            a2a_copy(slot).wait_recv()
+        group = xa.at[pl.ds(8, 8), 0] if phase else xa.at[pl.ds(1, 7), 0]
+        remote(group, group, a2a_s.at[0], a2a_r.at[phase], (above, ten)).wait_recv()
         ag_y(phase).start()
         ag_x(phase, 0, 0).start()
         ag_x(phase, 0, 1).start()
@@ -198,7 +192,6 @@
         ag_x(phase, row, phase).wait_recv()
         ag_far(phase, row).start()
 
-    ag_own(0)
 
     halo_delta.wait_recv()
     keep_d = jnp.where(con == 31, 0.0, 1.0).astype(F32)
@@ -211,7 +204,7 @@
     ga[0] = (backs * kv[...].astype(F32)).astype(BF16)
 
     def b_copy(index, source, target, device):
-        return remote(ga.at[source], ga.at[target], b_s.at[index], b_r.at[index], (device, ten))
+        return remote(ga.at[source], ga.at[target], b_s.at[0], b_r.at[index], (device, ten))
 
     up, down = at(z + 1, yl, core), at(z + 7, yl, core)
 
@@ -237,7 +230,6 @@
     across = b_copy(0, 0, 1, at(z, yl + 1, core))
     across.start()
 
-    ag_own(1)
 
     loads[7].wait()
 
@@ -249,7 +241,7 @@
 
     def c_remote(chunk, kind, src, dst, device):
         index = chunk * 8 + kind
-        return remote(src, dst, c_s.at[index], c_r.at[index], (con, device))
+        return remote(src, dst, c_s.at[0], c_r.at[index], (con, device))
 
     def y_copy(chunk):
         return c_remote(chunk, 0, tpart.at[1 - yh, :, :, ccols[chunk]], yr.at[:, :, ccols[chunk]], other)
@@ -335,11 +327,6 @@
             total = f32(tpart, yh, x, slice(None), cols) + f32(yr, x, slice(None), cols)
             ig[:, cols] = (total + f32(left_sum, chunk, 0) + f32(right_sum, chunk, 0)).astype(BF16)
 
-    def c_sent(chunk):
-        for kind in range(6):
-            x_copy(chunk, kind).wait_send()
-        (yx_copy if chunk in X_FIRST else y_copy)(chunk).wait_send()
-
     def filter_tile(l, carry):
         cols = lanes(l)
         rows = [iext[pl.ds(ROWS + 8 * i, 8), cols] for i in range(16)]
@@ -352,15 +339,19 @@
                 fpart[pl.ds(8 * a + r, 1), cols] = jnp.sum(total, axis=0, keepdims=True)
         return carry
 
+    ag_own(0)
     terms(0)
-    ag_other(0)
-    terms(1)
+    ag_own(1)
     forward(1, 0)
     across.wait_recv()
     right(1, 1).start()
     left(1, 1).start()
+    terms(1)
+    lax.fori_loop(0, 2, filter_tile, 0)
+    ag_other(0)
+    forward(2, 0)
     ag_forward(0, 0)
-    lax.fori_loop(0, 4, filter_tile, 0)
+    lax.fori_loop(2, 4, filter_tile, 0)
 
     half = CH // 2
     mine = pl.ds(pl.multiple_of(core * half, half), half)
@@ -368,32 +359,33 @@
     partner = (at(z, yl, core + 1), ten)
     f_core = remote(fpart.at[:, theirs], fcore, core_s.at[0], core_r.at[0], partner)
     f_core.start()
+    forward(1, 1)
     ag_other(1)
-    forward(2, 0)
     terms(2)
+
+    f_core.wait_recv()
+    fsum[...] = fpart[:, mine] + fcore[...]
+
+    def q_of(i, way):
+        return ((z + NZ + way * (i // 2)) % NZ) * 2 + (yl + i % 2) % 2
+
+    def rs_copy(i):
+        dest = q_of(i, 1)
+        return remote(
+            fsum.at[pl.ds(pl.multiple_of(dest * 8, 8), 8), :], frs.at[i], rs_s.at[0], rs_r.at[0], (dest * 2 + core, ten)
+        )
+
+    def rs_start(i, carry):
+        rs_copy(i).start()
+        return carry
+
+    lax.fori_loop(1, NQ, rs_start, 0)
+    forward(3, 0)
     c_pass_on(0)
     ag_forward(1, 0)
     ag_forward(0, 1)
-    forward(1, 1)
     terms(3)
-
-    f_core.wait_recv()
-    fsum[...] = fpart[:, mine] + fcore[...]
-
-    def q_of(i, way):
-        return ((z + NZ + way * (i // 2)) % NZ) * 2 + (yl + i % 2) % 2
-
-    def rs_copy(i):
-        dest = q_of(i, 1)
-        return remote(
-            fsum.at[pl.ds(pl.multiple_of(dest * 8, 8), 8), :], frs.at[i], rs_s.at[i], rs_r.at[i], (dest * 2 + core, ten)
-        )
-
-    def rs_start(i, carry):
-        rs_copy(i).start()
-        return carry
-
-    lax.fori_loop(1, NQ, rs_start, 0)
+    forward(2, 1)
 
     kgv[...] = (back[...].reshape(ROWS, CH) * vv[...].astype(F32)).astype(BF16)
     out_copies = [
@@ -428,14 +420,18 @@
         return carry
 
     c_sum_y(1)
-    forward(3, 0)
     lax.fori_loop(0, 2, mixed_tile, 0)
     ag_forward(1, 1)
-    forward(2, 1)
+    c_pass_on(1)
     lax.fori_loop(2, 4, mixed_tile, 0)
     copy = pltpu.make_async_copy(qgv, qg_hbm, out_sems.at[2])
     copy.start()
     out_copies.append(copy)
+
+    forward(3, 1)
+    if 0 in X_FIRST:
+        c_turn_y(0)
+    c_sum_y(2)
 
     far, other_far = ten_at(yh, x + 2), ten_at(yh + 1, x + 2)
     sources = (ten, other, x_down, x_up, ten_at(yh + 1, x + 3), ten_at(yh + 1, x + 1), far, other_far)
@@ -455,17 +451,9 @@
         else:
             wacc[cols, :] += new
 
-    if 0 in X_FIRST:
-        c_turn_y(0)
-    c_pass_on(1)
-    c_sum_y(2)
-    forward(3, 1)
-
-    def rs_wait(i, carry):
-        rs_copy(i).wait_recv()
-        return carry
-
-    lax.fori_loop(1, NQ, rs_wait, 0)
+    pieces = frs.at[pl.ds(1, NQ - 1)]
+    rs_all = remote(pieces, pieces, rs_s.at[0], rs_r.at[0], (above, ten))
+    rs_all.wait_recv()
     total = fsum[pl.ds(pl.multiple_of(q * 8, 8), 8), :]
     for i in range(1, NQ):
         total = total + frs[i]
@@ -474,7 +462,7 @@
 
     def fa_copy(i, source):
         ref = ffull.at[pl.ds(pl.multiple_of(source * 8, 8), 8), mine]
-        return remote(ref, ref, fa_s.at[i], fa_r.at[i], (q_of(i, 1) * 2 + core, ten))
+        return remote(ref, ref, fa_s.at[0], fa_r.at[0], (q_of(i, 1) * 2 + core, ten))
 
     def fa_start(i, carry):
         fa_copy(i, q).start()
@@ -503,13 +491,6 @@
     c_end(2)
     c_pass_on(3)
 
-    def fa_wait(i, carry):
-        fa_copy(i, q_of(i, -1)).wait_recv()
-        return carry
-
-    lax.fori_loop(1, NQ, fa_wait, 0)
-    f_back = remote(ffull.at[:, mine], ffull.at[:, mine], core_s.at[1], core_r.at[1], partner)
-    f_back.start()
     product(1, 0, 0)
     product(1, 0, 1)
     ag_x(1, 0, 0).wait_recv()
@@ -526,6 +507,23 @@
     w_core.start()
     product(1, 3, core)
 
+    fa_all = remote(pieces, pieces, fa_s.at[0], fa_r.at[0], (above, ten))
+    fa_all.wait_recv()
+    f_back = remote(ffull.at[:, mine], ffull.at[:, mine], core_s.at[1], core_r.at[1], partner)
+    f_back.start()
+    c_end(3)
+    copy = pltpu.make_async_copy(ig, ig_hbm, out_sems.at[5])
+    copy.start()
+    out_copies.append(copy)
+
+    w_core.wait_recv()
+    for n in range(4):
+        rows = pl.ds(64 * n, 64)
+        wout[rows, :] = wacc[pl.ds(pl.multiple_of(core * 256 + 64 * n, 64), 64), :] + wrecv[rows, :]
+        copy = pltpu.make_async_copy(wout.at[rows, :], wg_hbm.at[rows, :], out_sems.at[6 + n])
+        copy.start()
+        out_copies.append(copy)
+
     f_back_wait = remote(ffull.at[:, theirs], ffull.at[:, theirs], core_s.at[1], core_r.at[1], partner)
     f_back_wait.wait_recv()
     fgt[...] = ffull[...].T
@@ -537,45 +535,18 @@
         copy.start()
         out_copies.append(copy)
 
-    c_end(3)
-    copy = pltpu.make_async_copy(ig, ig_hbm, out_sems.at[5])
-    copy.start()
-    out_copies.append(copy)
-
-    w_core.wait_recv()
-    for n in range(4):
-        rows = pl.ds(64 * n, 64)
-        wout[rows, :] = wacc[pl.ds(pl.multiple_of(core * 256 + 64 * n, 64), 64), :] + wrecv[rows, :]
-        copy = pltpu.make_async_copy(wout.at[rows, :], wg_hbm.at[rows, :], out_sems.at[6 + n])
-        copy.start()
-        out_copies.append(copy)
-
     halo_delta.wait_send()
     halo_inner.wait_send()
 
-    def sent(i, carry):
-        rs_copy(i).wait_send()
-        fa_copy(i, q).wait_send()
-        return carry
-
-    lax.fori_loop(1, NQ, sent, 0)
-    for slot in range(1, NQ):
-        a2a_copy(slot).wait_send()
-    for phase in range(2):
-        ag_y(phase).wait_send()
-        for row in range(2):
-            ag_x(phase, row, 0).wait_send()
-            ag_x(phase, row, 1).wait_send()
-            ag_far(phase, row).wait_send()
-    across.wait_send()
-    for rel in range(2):
-        for d in range(1, 4):
-            right(d, rel).wait_send()
-            left(d, rel).wait_send()
-    right(4, 0).wait_send()
-    left(4, 1).wait_send()
-    for chunk in range(CHUNKS):
-        c_sent(chunk)
+    slots = xa.at[pl.ds(1, NQ - 1), 0]
+    remote(slots, slots, a2a_s.at[0], a2a_r.at[0], (above, ten)).wait_send()
+    seven = xa.at[:, pl.ds(0, NT - 1)]
+    remote(seven, seven, ag_s.at[0], ag_r.at[0], (above, ten)).wait_send()
+    remote(seven, seven, c_s.at[0], c_r.at[0], (above, ten)).wait_send()
+    blocks = ga.at[pl.ds(1, NQ - 1)]
+    remote(blocks, blocks, b_s.at[0], b_r.at[0], (above, ten)).wait_send()
+    rs_all.wait_send()
+    fa_all.wait_send()
     f_core.wait_send()
     f_back.wait_send()
     w_core.wait_send()
@@ -666,13 +637,13 @@
             dma((9,)),
             dma((10,)),
             dma((2,)), dma((2,)),
-            dma((NQ,)), dma((NQ,)),
-            dma((14,)), dma((14,)),
-            dma((17,)), dma((17,)),
-            dma((8 * CHUNKS,)), dma((8 * CHUNKS,)),
+            dma((1,)), dma((2,)),
+            dma((1,)), dma((14,)),
+            dma((1,)), dma((17,)),
+            dma((1,)), dma((8 * CHUNKS,)),
             dma((3,)), dma((3,)),
-            dma((NQ,)), dma((NQ,)),
-            dma((NQ,)), dma((NQ,)),
+            dma((1,)), dma((1,)),
+            dma((1,)), dma((1,)),
         ],
         compiler_params=pltpu.CompilerParams(
             collective_id=0, has_side_effects=True, vmem_limit_bytes=VMEM_LIMIT

time: 62 us -> 59.6 us (0.961)
  Pallas kernels: 61.3 us -> 58.8 us
    pallas_call x1, Pallas kernels: 58.9 us -> 56.5 us  [local(): pl.pallas_call(kernel, out_shape=(shape((ROWS, CH), BF16), shape((ROWS, C...]
where the time goes in v3:
time: 59.6 us; the launch traced here: 59.5 us
  Pallas kernels  58.8 us (99%)
  between operations  0.64 us (1%)
    pallas_call x1, Pallas kernels, local(): pl.pallas_call(kernel, out_shape=(shape((ROWS, CH), BF16), shape((ROWS, C...  56.5 us
    pallas_call x1, Pallas kernels, local(): pl.pallas_call(finish, out_shape=tuple((shape(out.shape, out.dtype) for o...  2.32 us

profile of v3, /device:TPU:1, one launch (start us, length us, event | category | flops | bytes accessed | tf_op | source)
XLA Modules:
  0.0 59.5 jit_solution(8415632096191248299)
XLA Ops:
  0.6 56.5 %hyena_back.1 = (bf16[128,512]{1,0:T(8,128)(2,1)}, bf16[128,512]{1,0:T(8,128)(2,1)}, bf16[128,512]{1,0:T(8,128)(2,1)}, f32[512,128]{1,0:T(8,128)}, f32[1,512]{1,...) custom-call(bf16[16,8192]{1,0:T(8,128)(2,1)} %x_hbm.1, bf16[128,512]{1,0:T(8,128)(2,1)} %q_hbm.1, ...), custom_call_target="tpu_custom_call" | custom-call | tf_op jit(solution)/shard_map/hyena_back/pallas_call | solution.py:580
  57.1 2.3 %finish.1 = (bf16[128,512]{1,0:T(8,128)(2,1)}, bf16[128,512]{1,0:T(8,128)(2,1)}, bf16[128,512]{1,0:T(8,128)(2,1)}, f32[512,128]{1,0:T(8,128)}, f32[1,512]{1,0:T(...) custom-call(bf16[128,512]{1,0:T(8,128)(2,1)} %get-tuple-element.21.refs_0_, ...), custom_call_target="tpu_custom_call" | custom-call | tf_op jit(solution)/shard_map/finish/pallas_call | solution.py:656

commit v4 on v3

--- a/solution.py
+++ b/solution.py
@@ -107,7 +107,7 @@
             (dest * 2 + core, ten),
         )
 
-    for slot in range(1, NQ):
+    for slot in (14, 15, 10, 11, 12, 13, 6, 7, 8, 9, 2, 3, 4, 5, 1):
         a2a_copy(slot).start()
     halo_inner.start()
 

time: 59.6 us -> 59.3 us (level)
  no operation moved by 1% of the time
where the time goes in v4:
time: 59.3 us; the launch traced here: 59.1 us
  Pallas kernels  58.5 us (99%)
  between operations  0.64 us (1%)
    pallas_call x1, Pallas kernels, local(): pl.pallas_call(kernel, out_shape=(shape((ROWS, CH), BF16), shape((ROWS, C...  56.2 us
    pallas_call x1, Pallas kernels, local(): pl.pallas_call(finish, out_shape=tuple((shape(out.shape, out.dtype) for o...  2.32 us

profile of v4, /device:TPU:1, one launch (start us, length us, event | category | flops | bytes accessed | tf_op | source)
XLA Modules:
  0.0 59.1 jit_solution(10504609246505407521)
XLA Ops:
  0.6 56.2 %hyena_back.1 = (bf16[128,512]{1,0:T(8,128)(2,1)}, bf16[128,512]{1,0:T(8,128)(2,1)}, bf16[128,512]{1,0:T(8,128)(2,1)}, f32[512,128]{1,0:T(8,128)}, f32[1,512]{1,...) custom-call(bf16[16,8192]{1,0:T(8,128)(2,1)} %x_hbm.1, bf16[128,512]{1,0:T(8,128)(2,1)} %q_hbm.1, ...), custom_call_target="tpu_custom_call" | custom-call | tf_op jit(solution)/shard_map/hyena_back/pallas_call | solution.py:580
  56.8 2.3 %finish.1 = (bf16[128,512]{1,0:T(8,128)(2,1)}, bf16[128,512]{1,0:T(8,128)(2,1)}, bf16[128,512]{1,0:T(8,128)(2,1)}, f32[512,128]{1,0:T(8,128)}, f32[1,512]{1,0:T(...) custom-call(bf16[128,512]{1,0:T(8,128)(2,1)} %get-tuple-element.21.refs_0_, ...), custom_call_target="tpu_custom_call" | custom-call | tf_op jit(solution)/shard_map/finish/pallas_call | solution.py:656
